TPU v7x, 256 devices: a whole 4x4x8 slice. The times are simulated.
256 devices in a mesh: grp: 4 (over y), dev: 64 (over x, z, core).
Axes of the slice: x: 4, y: 4, z: 8, core: 2. Of those that a mesh axis runs over, the one named last changes fastest.
Arguments:
- embeds: bfloat16 [524288, 512], P(('grp', 'dev')), may hold values from -6 to 6
- cluster: int32 [524288, 1], P(('grp', 'dev')), may hold values from 0 to 511; in each aligned block of 2048 rows (0 to 2047, 2048 to 4095, ...) at most 6 rows name the same one
Outputs:
- nearest: float32 [524288], P(('grp', 'dev'))
Inputs may be any that keep to these rules, and one draw needn't show every extreme that they name: The rows of one device name any one cluster at most 6 times, a bound that some block reaches.
All inputs are finite; a program needn't handle non-finite values.
Results may differ from a plain program's by a relative error of at most 0.0013.
Values may be sent and summed in bfloat16 or wider, within the bound.
A program may use at most 64 MiB of HBM per device.

v0:
```python
import jax
import jax.numpy as jnp
from jax import lax
from jax.sharding import PartitionSpec as P


def on_device(embeds, cluster):
    row_count, feat_count = embeds.shape
    grp_count = lax.axis_size("grp")
    dev_count = lax.axis_size("dev")
    device_count = grp_count * dev_count
    clusters_per = max(1, 2 * row_count // (8 * device_count))
    cap_slots = 3 * row_count // (2 * clusters_per * device_count)
    slot_count = clusters_per * cap_slots
    floats = embeds.astype(jnp.float32)
    unit_rows = (
        floats * lax.rsqrt(jnp.sum(floats * floats, axis=1, keepdims=True) + 1e-06)
    ).astype(jnp.bfloat16)
    cluster_ids = cluster[:, 0]
    owner_ids = cluster_ids // clusters_per
    sub_ids = cluster_ids % clusters_per
    same_cluster = cluster_ids[:, None] == cluster_ids[None, :]
    earlier = lax.broadcasted_iota(jnp.int32, (row_count, row_count), 1) < lax.broadcasted_iota(
        jnp.int32, (row_count, row_count), 0
    )
    rank_in = jnp.sum((same_cluster & earlier).astype(jnp.int32), axis=1)
    target = owner_ids * slot_count + sub_ids * cap_slots + rank_in
    send_rows = (
        jnp.zeros((device_count * slot_count, feat_count), jnp.bfloat16).at[target].set(unit_rows)
    )
    send_rows = send_rows.reshape(grp_count, dev_count, slot_count, feat_count)
    all_ids = jnp.arange(device_count * clusters_per, dtype=jnp.int32)
    send_counts = jnp.sum((cluster_ids[:, None] == all_ids[None, :]).astype(jnp.int32), axis=0)
    send_counts = send_counts.reshape(grp_count, dev_count, clusters_per)
    got_rows, got_counts = (
        lax.all_to_all(
            lax.all_to_all(send_rows, "grp", split_axis=0, concat_axis=0, tiled=True),
            "dev",
            split_axis=1,
            concat_axis=1,
            tiled=True,
        ),
        lax.all_to_all(
            lax.all_to_all(send_counts, "grp", split_axis=0, concat_axis=0, tiled=True),
            "dev",
            split_axis=1,
            concat_axis=1,
            tiled=True,
        ),
    )
    total_slots = device_count * slot_count
    flat_rows = got_rows.reshape(total_slots, feat_count)
    is_live = (
        jnp.arange(cap_slots, dtype=jnp.int32)[None, None, None, :] < got_counts[..., None]
    ).reshape(total_slots)
    sub_grid = jnp.broadcast_to(
        jnp.arange(clusters_per, dtype=jnp.int32)[None, None, :, None],
        (grp_count, dev_count, clusters_per, cap_slots),
    ).reshape(total_slots)
    key_ids = jnp.where(is_live, sub_grid, -1)
    slot_index = jnp.arange(total_slots, dtype=jnp.int32)
    block_rows_n = 768
    block_count = total_slots // block_rows_n

    def tile_max(pieces):
        block_rows, block_keys, block_slots = pieces
        sims = lax.dot_general(
            block_rows, flat_rows, (((1,), (1,)), ((), ())), preferred_element_type=jnp.float32
        )
        keep_pair = (
            (block_keys[:, None] == key_ids[None, :])
            & (block_keys[:, None] >= 0)
            & (block_slots[:, None] != slot_index[None, :])
        )
        return jnp.max(jnp.where(keep_pair, sims, jnp.float32(-1.0)), axis=1)

    best_sim = lax.map(
        tile_max,
        (
            flat_rows.reshape(block_count, block_rows_n, feat_count),
            key_ids.reshape(block_count, block_rows_n),
            slot_index.reshape(block_count, block_rows_n),
        ),
    )
    best_sim = best_sim.reshape(grp_count, dev_count, slot_count)
    returned = lax.all_to_all(
        lax.all_to_all(best_sim, "grp", split_axis=0, concat_axis=0, tiled=True),
        "dev",
        split_axis=1,
        concat_axis=1,
        tiled=True,
    )
    return returned.reshape(total_slots)[target]


def solution(mesh):
    in_specs = (P(("grp", "dev"), None), P(("grp", "dev"), None))
    out_specs = P(("grp", "dev"))
    return jax.shard_map(
        on_device, mesh=mesh, in_specs=in_specs, out_specs=out_specs, check_vma=False
    )
```

profile of v0, /device:TPU:1, one launch (start us, length us, event | category | flops | bytes accessed | tf_op | source)
XLA Modules:
  0.0 263.8 jit_solution(7100244932787288316)
XLA Ops:
  0.0 1.3 convert_reduce_fusion.1
  1.3 0.1 reshape.57
  1.4 0.1 copy.18
  1.5 0.7 reshape.88
  2.2 5.0 %all-to-all-start = ((s32[4,1,128]{2,1,0:T(1,128)}), s32[4,1,128]{2,1,0:T(1,128)S(1)}, u32[]{:S(2)}, u32[]{:S(2)}) async-start(s32[4,1,128]{2,1,0:T(1,128)} %reshape.88), calls=%async_computation | async-start | bytes 4096 | tf_op jit(solution)/shard_map/all_to_all | solution.py:44
  7.2 5.2 %convert_reduce_fusion = s32[2048]{0:T(1024)S(1)} fusion(s32[2048]{0:T(1024)} %bitcast.24), kind=kLoop, calls=%fused_computation.14 | loop fusion | flops 20969472 | bytes 16384 | tf_op jit(solution)/shard_map/reduce_sum | solution.py:26
  12.4 0.8 compare_select_fusion.1
  13.2 0.0 copy-start
  13.2 2.1 fusion.9
  15.3 11.8 %scatter_custom_fusion = bf16[3072,512]{1,0:T(8,128)(2,1)S(1)} fusion(s32[2048]{0:T(1024)S(1)} %bitcast.19, bf16[2048,512]{1,0:T(8,128)(2,1)} %param.4, f32[2048]{0:T(1024)S(1)} %add_rsqrt_fusion, bf16[]{:T(256)} %constant.52.clone.1), kind=kCustom, calls=%fused_computation.23 | custom fusion | flops 3145728 | bytes 5251074 | tf_op jit(solution)/shard_map/scatter | solution.py:29
  27.1 0.0 copy-done
  27.1 2.7 %reshape.61 = bf16[4,64,12,512]{3,2,1,0:T(8,128)(2,1)} reshape(bf16[3072,512]{1,0:T(8,128)(2,1)S(1)} %scatter_custom_fusion) | data formatting | bytes 6291456 | tf_op jit(solution)/shard_map/reshape | solution.py:31
  29.8 5.6 %copy.21 = bf16[4,64,12,512]{3,1,2,0:T(8,128)(2,1)} copy(bf16[4,64,12,512]{3,2,1,0:T(8,128)(2,1)} %reshape.61) | data formatting | bytes 6291456 | tf_op jit(solution)/shard_map/reshape | solution.py:31
  35.4 0.0 all-to-all-done
  35.4 4.2 %all-to-all-start.2 = ((bf16[4,64,12,512]{3,1,2,0:T(8,128)(2,1)}), bf16[4,64,12,512]{3,1,2,0:T(8,128)(2,1)S(1)}, u32[]{:S(2)}, u32[]{:S(2)}) async-start(bf16[4,64,12,512]{3,1,2,0:T(8,128)(2,1)} %copy.21), calls=%async_computation.2 | async-start | bytes 6291456 | tf_op jit(solution)/shard_map/all_to_all | solution.py:37
  39.7 0.6 broadcast.68
  40.3 0.7 reduce.4
  41.0 0.1 reshape.89
  41.0 0.7 copy.19
  41.8 33.5 %all-to-all-done.2 = bf16[4,64,12,512]{3,1,2,0:T(8,128)(2,1)S(1)} async-done(((bf16[4,64,12,512]{3,1,2,0:T(8,128)(2,1)}), bf16[4,64,12,512]{3,1,2,0:T(8,128)(2,1)S(1)}, u32[]{:S(2)}, u32[]{:S(2)}) %all-to-all-start.2) | async-done | bytes 3145760 | tf_op jit(solution)/shard_map/all_to_all | solution.py:37
  75.3 14.4 %all-to-all-start.1 = ((s32[4,64,2]{0,2,1:T(2,128)}), s32[4,64,2]{0,2,1:T(2,128)S(1)}, u32[]{:S(2)}, u32[]{:S(2)}) async-start(s32[4,64,2]{0,2,1:T(2,128)} %copy.19), calls=%async_computation.1 | async-start | bytes 131072 | tf_op jit(solution)/shard_map/all_to_all | solution.py:43
  89.7 4.1 %copy.22 = bf16[4,64,12,512]{3,0,2,1:T(4,128)(2,1)} copy(bf16[4,64,12,512]{3,1,2,0:T(8,128)(2,1)S(1)} %all-to-all-done.2) | data formatting | bytes 6291456 | tf_op jit(solution)/shard_map/all_to_all | solution.py:37
  93.8 5.7 %all-to-all-done.1 = s32[4,64,2]{0,2,1:T(2,128)S(1)} async-done(((s32[4,64,2]{0,2,1:T(2,128)}), s32[4,64,2]{0,2,1:T(2,128)S(1)}, u32[]{:S(2)}, u32[]{:S(2)}) %all-to-all-start.1) | async-done | bytes 2080 | tf_op jit(solution)/shard_map/all_to_all | solution.py:43
  99.4 4.7 %all-to-all-start.3 = ((bf16[4,64,12,512]{3,0,2,1:T(4,128)(2,1)}), bf16[4,64,12,512]{3,0,2,1:T(4,128)(2,1)S(1)}, u32[]{:S(2)}, u32[]{:S(2)}) async-start(bf16[4,64,12,512]{3,0,2,1:T(4,128)(2,1)} %copy.22), calls=%async_computation.3 | async-start | bytes 6291456 | tf_op jit(solution)/shard_map/all_to_all | solution.py:36
  104.2 0.1 broadcast_in_dim.45
  104.3 0.7 lt.44
  105.1 0.6 copy.20
  105.6 0.3 lt.46
  106.0 0.9 lt.47
  106.9 0.7 compare_select_fusion.5
  107.6 70.0 %all-to-all-done.3 = bf16[4,64,12,512]{3,0,2,1:T(4,128)(2,1)S(1)} async-done(((bf16[4,64,12,512]{3,0,2,1:T(4,128)(2,1)}), bf16[4,64,12,512]{3,0,2,1:T(4,128)(2,1)S(1)}, u32[]{:S(2)}, u32[]{:S(2)}) %all-to-all-start.3) | async-done | bytes 3145760 | tf_op jit(solution)/shard_map/all_to_all | solution.py:36
  177.6 2.9 %copy.23 = bf16[4,64,12,512]{3,2,1,0:T(8,128)(2,1)} copy(bf16[4,64,12,512]{3,0,2,1:T(4,128)(2,1)S(1)} %all-to-all-done.3) | data formatting | bytes 6291456 | tf_op jit(solution)/shard_map/all_to_all | solution.py:36
  180.5 6.2 %reshape.62 = bf16[3072,512]{1,0:T(8,128)(2,1)} reshape(bf16[4,64,12,512]{3,2,1,0:T(8,128)(2,1)} %copy.23) | data formatting | bytes 6291456 | tf_op jit(solution)/shard_map/reshape | solution.py:52
  186.7 2.3 copy.24
  189.0 0.0 copy-done.2
  189.0 27.4 %while.11 = (s32[]{:T(128)}, f32[4,768]{1,0:T(4,128)S(1)}, s32[4,768]{1,0:T(4,128)S(1)}, s32[4,768]{1,0:T(4,128)S(1)}, bf16[4,768,512]{2,1,0:T(8,128)(2,1)}, /*i...) while((s32[]{:T(128)}, f32[4,768]{1,0:T(4,128)S(1)}, ...), condition=%wide.region_6.7_spmd.clone, body=%wide.region_4.6_spmd.clone.sunk | while | flops 2430081024 | bytes 4022373 | solution.py:77
  189.0 0.3 compare_select_fusion.7
  189.4 0.3 select_n.71
  189.7 6.1 %select_reduce_fusion.2 = f32[768]{0:T(1024)S(1)} fusion(bf16[3072,512]{1,0:T(8,128)(2,1)} %get-tuple-element.173, s32[768]{0:T(1024)S(1)} %get-tuple-element.148, s32[3072]{0:T(1024)S(1)} %select_n.71, s32[768]{0:T(1024)S(1)} %get-tuple-element.149, pred[768]{0:T(1024)(128)(4,1)S(1)} %broadcast_compare_fusion.2, ...), kind=kOutput, calls=%fused_computation.5.clone.1 | convolution fusion | flops 2430074112 | bytes 3954944 | tf_op jit(solution)/shard_map/while/body/eval_jaxpr/dot_general | solution.py:67
  195.8 0.1 dynamic_update_slice.6
  195.9 0.3 compare_select_fusion.7
  196.2 0.3 select_n.71
  196.6 6.1 %select_reduce_fusion.2 = f32[768]{0:T(1024)S(1)} fusion(bf16[3072,512]{1,0:T(8,128)(2,1)} %get-tuple-element.173, s32[768]{0:T(1024)S(1)} %get-tuple-element.148, s32[3072]{0:T(1024)S(1)} %select_n.71, s32[768]{0:T(1024)S(1)} %get-tuple-element.149, pred[768]{0:T(1024)(128)(4,1)S(1)} %broadcast_compare_fusion.2, ...), kind=kOutput, calls=%fused_computation.5.clone.1 | convolution fusion | flops 2430074112 | bytes 3954944 | tf_op jit(solution)/shard_map/while/body/eval_jaxpr/dot_general | solution.py:67
  202.6 0.1 dynamic_update_slice.6
  202.8 0.3 compare_select_fusion.7
  203.1 0.3 select_n.71
  203.4 6.1 %select_reduce_fusion.2 = f32[768]{0:T(1024)S(1)} fusion(bf16[3072,512]{1,0:T(8,128)(2,1)} %get-tuple-element.173, s32[768]{0:T(1024)S(1)} %get-tuple-element.148, s32[3072]{0:T(1024)S(1)} %select_n.71, s32[768]{0:T(1024)S(1)} %get-tuple-element.149, pred[768]{0:T(1024)(128)(4,1)S(1)} %broadcast_compare_fusion.2, ...), kind=kOutput, calls=%fused_computation.5.clone.1 | convolution fusion | flops 2430074112 | bytes 3954944 | tf_op jit(solution)/shard_map/while/body/eval_jaxpr/dot_general | solution.py:67
  209.5 0.1 dynamic_update_slice.6
  209.6 0.3 compare_select_fusion.7
  210.0 0.3 select_n.71
  210.3 6.1 %select_reduce_fusion.2 = f32[768]{0:T(1024)S(1)} fusion(bf16[3072,512]{1,0:T(8,128)(2,1)} %get-tuple-element.173, s32[768]{0:T(1024)S(1)} %get-tuple-element.148, s32[3072]{0:T(1024)S(1)} %select_n.71, s32[768]{0:T(1024)S(1)} %get-tuple-element.149, pred[768]{0:T(1024)(128)(4,1)S(1)} %broadcast_compare_fusion.2, ...), kind=kOutput, calls=%fused_computation.5.clone.1 | convolution fusion | flops 2430074112 | bytes 3954944 | tf_op jit(solution)/shard_map/while/body/eval_jaxpr/dot_general | solution.py:67
  216.4 0.1 dynamic_update_slice.6
  216.5 0.1 reshape.63
  216.6 0.1 copy.26
  216.7 0.1 reshape.90
  216.8 6.5 %all_to_all.30 = f32[4,1,768]{2,1,0:T(1,128)S(1)} all-to-all(f32[4,1,768]{2,1,0:T(1,128)S(1)} %reshape.90), channel_id=1, replica_groups=mesh['grp'=4,'dev'=64] {'grp'}, dimensions={0} | all-to-all | bytes 24576 | tf_op jit(solution)/shard_map/all_to_all | solution.py:87
  223.3 0.6 broadcast.69
  223.9 0.7 reduce.5
  224.7 0.1 reshape.91
  224.7 0.8 copy.27
  225.5 7.2 %all-to-all-start.5 = ((f32[4,64,12]{2,0,1:T(4,128)}), f32[4,64,12]{2,0,1:T(4,128)S(1)}, u32[]{:S(2)}, u32[]{:S(2)}) async-start(f32[4,64,12]{2,0,1:T(4,128)} %copy.27), calls=%async_computation.5 | async-start | bytes 262144 | tf_op jit(solution)/shard_map/all_to_all | solution.py:86
  232.8 10.3 %all-to-all-done.5 = f32[4,64,12]{2,0,1:T(4,128)S(1)} async-done(((f32[4,64,12]{2,0,1:T(4,128)}), f32[4,64,12]{2,0,1:T(4,128)S(1)}, u32[]{:S(2)}, u32[]{:S(2)}) %all-to-all-start.5) | async-done | bytes 12320 | tf_op jit(solution)/shard_map/all_to_all | solution.py:86
  243.1 0.1 reshape.64
  243.2 20.5 %gather_fusion = f32[2048]{0:T(1024)} fusion(f32[3072]{0:T(1024)S(1)} %reshape.64, s32[2048]{0:T(1024)S(1)} %broadcast_clamp_fusion), kind=kCustom, calls=%fused_computation | custom fusion | bytes 24576 | tf_op jit(solution)/shard_map/gather | solution.py:93
  (22 shorter events, 0.2 us)
Async XLA Ops:
  2.2 33.2 %all-to-all-start = ((s32[4,1,128]{2,1,0:T(1,128)}), s32[4,1,128]{2,1,0:T(1,128)S(1)}, u32[]{:S(2)}, u32[]{:S(2)}) async-start(s32[4,1,128]{2,1,0:T(1,128)} %reshape.88), calls=%async_computation | async-start | bytes 4096 | tf_op jit(solution)/shard_map/all_to_all | solution.py:44
  13.2 13.9 %copy-start = (s32[2048,1]{0,1:T(1,128)}, s32[2048,1]{0,1:T(1,128)S(1)}, u32[]{:S(2)}) copy-start(s32[2048,1]{0,1:T(1,128)S(1)} %compare_select_fusion.1) | copy-start | bytes 24580
  35.4 39.8 %all-to-all-start.2 = ((bf16[4,64,12,512]{3,1,2,0:T(8,128)(2,1)}), bf16[4,64,12,512]{3,1,2,0:T(8,128)(2,1)S(1)}, u32[]{:S(2)}, u32[]{:S(2)}) async-start(bf16[4,64,12,512]{3,1,2,0:T(8,128)(2,1)} %copy.21), calls=%async_computation.2 | async-start | bytes 6291456 | tf_op jit(solution)/shard_map/all_to_all | solution.py:37
  75.3 24.2 %all-to-all-start.1 = ((s32[4,64,2]{0,2,1:T(2,128)}), s32[4,64,2]{0,2,1:T(2,128)S(1)}, u32[]{:S(2)}, u32[]{:S(2)}) async-start(s32[4,64,2]{0,2,1:T(2,128)} %copy.19), calls=%async_computation.1 | async-start | bytes 131072 | tf_op jit(solution)/shard_map/all_to_all | solution.py:43
  99.4 78.2 %all-to-all-start.3 = ((bf16[4,64,12,512]{3,0,2,1:T(4,128)(2,1)}), bf16[4,64,12,512]{3,0,2,1:T(4,128)(2,1)S(1)}, u32[]{:S(2)}, u32[]{:S(2)}) async-start(bf16[4,64,12,512]{3,0,2,1:T(4,128)(2,1)} %copy.22), calls=%async_computation.3 | async-start | bytes 6291456 | tf_op jit(solution)/shard_map/all_to_all | solution.py:36
  186.7 2.3 copy-start.2
  189.0 43.8 %copy-start.1 = (s32[2048,1]{0,1:T(1,128)S(1)}, s32[2048,1]{0,1:T(1,128)}, u32[]{:S(2)}) copy-start(s32[2048,1]{0,1:T(1,128)} %copy-done) | copy-start | bytes 24580
  225.5 17.6 %all-to-all-start.5 = ((f32[4,64,12]{2,0,1:T(4,128)}), f32[4,64,12]{2,0,1:T(4,128)S(1)}, u32[]{:S(2)}, u32[]{:S(2)}) async-start(f32[4,64,12]{2,0,1:T(4,128)} %copy.27), calls=%async_computation.5 | async-start | bytes 262144 | tf_op jit(solution)/shard_map/all_to_all | solution.py:86
where the time goes:
time: 265 us; the launch traced here: 264 us
  waiting for transfers between devices  119 us (45%)
  local copies, waits for them, and re-layouts  53 us (20%)
  starting transfers between devices  35.6 us (13%)
  other arithmetic  24.6 us (9%)
  matrix products  24.2 us (9%)
  blocking collectives  6.53 us (2%)
    all_to_all x1, waiting for transfers between devices, on_device(): lax.all_to_all(lax.all_to_all(send_rows, 'grp', split_axis=0, concat_axis...  70 us
    all_to_all x1, waiting for transfers between devices, on_device(): lax.all_to_all(send_rows, 'grp', split_axis=0, concat_axis=0, tiled=True)  33.5 us
    dot_general x4, matrix products, tile_max(): lax.dot_general(block_rows, flat_rows, (((1,), (1,)), ((), ())), preferre...  24.2 us
    gather x1, local copies, waits for them, and re-layouts, on_device(): return returned.reshape(total_slots)[target]  20.5 us
    all_to_all x1, starting transfers between devices, on_device(): lax.all_to_all(lax.all_to_all(send_counts, 'grp', split_axis=0, concat_ax...  14.4 us
    scatter x1, other arithmetic, on_device(): jnp.zeros((device_count * slot_count, feat_count), jnp.bfloat16).at[target]  11.8 us
    all_to_all x1, waiting for transfers between devices, on_device(): lax.all_to_all(lax.all_to_all(best_sim, 'grp', split_axis=0, concat_axis=...  10.3 us
    reshape x2, local copies, waits for them, and re-layouts, on_device(): send_rows = send_rows.reshape(grp_count, dev_count, slot_count, feat_count)  8.33 us
  transfers between devices with their start and end apart: 5, of which 4 were waited for; matrix products, arithmetic and copies ran while one was open for 14% of the time, Pallas kernels for 0%

commit v1 on v0

v1 whole, which is shorter than its diff:
```python
import functools

import jax
import jax.numpy as jnp
from jax import lax
from jax.experimental import pallas as pl
from jax.experimental.pallas import tpu as pltpu
from jax.sharding import PartitionSpec as P

LOGICAL = pl.DeviceIdType.LOGICAL
NY, NX, NZ, NC = 4, 4, 8, 2
N_DEV = NY * NX * NZ * NC
ROWS, FEAT = 2048, 512
OWN, CAP = 2, 6
N_CL = OWN * N_DEV
GROUP = NZ * NC
CHUNKS = N_DEV // GROUP
SLOTS = GROUP * CAP
STRIDE = 128
MSG_R, MSG_C = 16, 384
HEAD = 384
DEAD = 4.0
FAR = -1e6


def iota(shape, dim):
    return lax.broadcasted_iota(jnp.int32, shape, dim)


def ones_at(mask):
    return jnp.where(mask, 1.0, 0.0).astype(jnp.bfloat16)


def dot(a, b):
    return jnp.dot(a, b, preferred_element_type=jnp.float32)


def dot_t(a, b):
    return lax.dot_general(a, b, (((1,), (1,)), ((), ())), preferred_element_type=jnp.float32)


def split3(v):
    hi = v.astype(jnp.bfloat16)
    rest = v - hi.astype(jnp.float32)
    mid = rest.astype(jnp.bfloat16)
    lo = (rest - mid.astype(jnp.float32)).astype(jnp.bfloat16)
    return hi, mid, lo


def kernel(
    ids_ref, embeds_hbm, out_ref,
    embeds, send, recv, unit, bias, best, rank, place, pick,
    pack, unpack, ret_out, ret_in,
    load_sem, sent_sem, got_sem, in_sem, back_sent_sem, back_got_sem,
):
    my_y = lax.axis_index("grp")
    my_dev = lax.axis_index("dev")
    my_x = my_dev // (NZ * NC)
    my_z = (my_dev // NC) % NZ
    my_c = my_dev % NC

    load = pltpu.make_async_copy(embeds_hbm, embeds, load_sem)
    load.start()

    def plane(sign):
        return [
            (my_z + sign * (j % NZ) + NZ) % NZ * NC + (my_c + j // NZ) % NC for j in range(GROUP)
        ]

    def column(g, sign):
        y = (my_y + sign * (g // NX) + NY) % NY
        x = (my_x + sign * (g % NX) + NX) % NX
        return (y * NX + x) * (NZ * NC)

    near = plane(1)
    here = column(0, 1)

    barrier = pltpu.get_barrier_semaphore()
    for j in range(1, GROUP):
        pl.semaphore_signal(barrier, inc=1, device_id=here + near[j], device_id_type=LOGICAL)
    for g in range(1, CHUNKS):
        pl.semaphore_signal(
            barrier, inc=1, device_id=column(g, 1) + near[0], device_id_type=LOGICAL
        )

    tri = ones_at(
        (iota((128, 256), 0) < iota((128, 256), 1)) | (iota((128, 256), 1) >= 128)
    )

    def rank_block(b, seen):
        at = pl.ds(pl.multiple_of(b * 128, 128), 128)
        member = iota((N_CL, 128), 0) == ids_ref[:, at]
        sums = dot(ones_at(member), tri)
        rank[:, at] = jnp.sum(
            jnp.where(member, sums[:, :128] + seen, 0.0), axis=0, keepdims=True
        )
        return seen + sums[:, 128:]

    lax.fori_loop(0, ROWS // 128, rank_block, jnp.zeros((N_CL, 128), jnp.float32))

    ids = ids_ref[...]
    ranks = rank[...].astype(jnp.int32)
    owner = ids >> 1
    sub = ids & 1
    dy = ((owner >> 6) - my_y) & (NY - 1)
    dx = ((owner >> 4) - my_x) & (NX - 1)
    dz = ((owner >> 1) - my_z) & (NZ - 1)
    dc = (owner - my_c) & (NC - 1)
    chunk = dy * NX + dx
    member_of = dc * NZ + dz
    slot = sub * SLOTS + member_of * CAP + ranks
    place[...] = chunk * (OWN * SLOTS) + slot

    def block_matrix(rows, slots_dim, which):
        block = iota(rows, 1 - slots_dim)
        s = iota(rows, slots_dim)
        peer = block // MSG_R
        i = block % MSG_R
        if which == 0:
            q, ok = i, i < OWN * CAP
        else:
            q, ok = 3 * (i - OWN * CAP) + (which - 1), i >= OWN * CAP
        return peer, q, ok, s

    for which in range(4):
        peer, q, ok, s = block_matrix((GROUP * MSG_R, OWN * SLOTS), 1, which)
        pack[which] = ones_at(ok & (s == (q // CAP) * SLOTS + peer * CAP + q % CAP))
        peer, q, ok, s = block_matrix((OWN * STRIDE, GROUP * MSG_R), 0, which)
        unpack[which] = ones_at(ok & (s == (q // CAP) * STRIDE + peer * CAP + q % CAP))

    pl.semaphore_wait(barrier, GROUP - 1 + CHUNKS - 1)
    for g in range(1, CHUNKS):
        pl.semaphore_signal(in_sem, inc=1, device_id=column(g, 1) + near[0], device_id_type=LOGICAL)
    pl.semaphore_wait(in_sem, CHUNKS - 1)
    load.wait()

    def make_chunk(g):
        hit = iota((OWN * SLOTS, ROWS), 0) == place[...] - g * (OWN * SLOTS)
        chosen = jnp.where(hit, 1.0, 0.0)
        live = jnp.sum(chosen, axis=1, keepdims=True)
        rows = dot(chosen.astype(jnp.bfloat16), embeds[...])
        rows = rows * lax.rsqrt(jnp.sum(rows * rows, axis=1, keepdims=True) + 1e-06)
        first = (iota((OWN * SLOTS, FEAT), 1) == 0) & (live < 0.5)
        rows = jnp.where(first, DEAD, rows).astype(jnp.bfloat16)
        tail = rows[:, HEAD:]
        for c in range(3):
            lanes = slice(c * 128, (c + 1) * 128)
            block = dot(pack[0], rows[:, lanes]) + dot(pack[1 + c], tail)
            send[pl.ds(g * GROUP, GROUP), :, lanes] = block.astype(jnp.bfloat16).reshape(
                GROUP, MSG_R, 128
            )

    def send_chunk(g, first):
        base = column(g, 1)
        for j in range(first, GROUP):
            k = g * GROUP + j
            pltpu.make_async_remote_copy(
                src_ref=send.at[k], dst_ref=recv.at[k], send_sem=sent_sem, recv_sem=got_sem.at[g],
                device_id=base + near[j], device_id_type=LOGICAL,
            ).start()

    make_chunk(0)
    send_chunk(0, 1)
    pltpu.make_async_copy(send.at[0], recv.at[0], got_sem.at[0]).start()

    def send_step(g, carry):
        make_chunk(g)
        send_chunk(g, 0)
        return carry

    lax.fori_loop(1, CHUNKS, send_step, 0)

    for s in range(OWN):
        unit[s] = jnp.zeros((CHUNKS * STRIDE, FEAT), jnp.bfloat16)
        bias[s] = jnp.full((CHUNKS * STRIDE, 128), FAR, jnp.float32)
        best[s] = jnp.full((1, CHUNKS * STRIDE), -1.0, jnp.float32)
    pick[...] = ones_at(iota((N_DEV, ROWS), 0) == chunk * GROUP + member_of)

    def got_step(g, carry):
        mine = pl.ds(g * GROUP, GROUP)
        pltpu.make_async_copy(recv.at[mine], recv.at[mine], got_sem.at[g]).wait()
        block = recv[mine].reshape(GROUP * MSG_R, MSG_C)
        head = dot(unpack[0], block)
        tail = (
            dot(unpack[1], block[:, :128])
            + dot(unpack[2], block[:, 128:256])
            + dot(unpack[3], block[:, 256:])
        )
        at = pl.ds(pl.multiple_of(g * STRIDE, STRIDE), STRIDE)
        for s in range(OWN):
            part = slice(s * STRIDE, (s + 1) * STRIDE)
            new = jnp.concatenate([head[part], tail[part]], axis=1).astype(jnp.bfloat16)
            empty = (head[part, :1] > 2.0) | (iota((STRIDE, 1), 0) >= SLOTS)
            new_bias = jnp.where(empty, FAR, 0.0)
            held = unit[s]
            by_old = jnp.max(dot_t(held, new) + bias[s], axis=0, keepdims=True)
            by_new = jnp.max(dot_t(new, held) + new_bias, axis=0, keepdims=True)
            among = dot_t(new, new) + new_bias
            among = jnp.where(
                iota((STRIDE, STRIDE), 0) == iota((STRIDE, STRIDE), 1), -1.0, among
            )
            arrived = iota((1, CHUNKS * STRIDE), 1) < g * STRIDE
            best[s] = jnp.maximum(best[s], jnp.where(arrived, by_new, -1.0))
            best[s, :, at] = jnp.maximum(
                jnp.maximum(by_old, jnp.max(among, axis=0, keepdims=True)), -1.0
            )
            unit[s, at] = new
            bias[s, at] = jnp.broadcast_to(new_bias, (STRIDE, 128))
        return carry

    lax.fori_loop(0, CHUNKS, got_step, 0)

    far = plane(-1)
    for s in range(OWN):
        for g in range(CHUNKS):
            ret_out[g, s : s + 1] = best[s, :, g * STRIDE : (g + 1) * STRIDE]

    def return_chunk(g, first):
        base = column(g, -1)
        for j in range(first, GROUP):
            pltpu.make_async_remote_copy(
                src_ref=ret_out.at[g], dst_ref=ret_in.at[g * GROUP + j],
                send_sem=back_sent_sem, recv_sem=back_got_sem,
                device_id=base + far[j], device_id_type=LOGICAL,
            ).start()

    pltpu.make_async_copy(ret_out.at[0], ret_in.at[0], back_got_sem).start()
    return_chunk(0, 1)

    def return_step(g, carry):
        return_chunk(g, 0)
        return carry

    lax.fori_loop(1, CHUNKS, return_step, 0)
    pltpu.make_async_copy(ret_in, ret_in, back_got_sem).wait()

    wanted = (iota((N_DEV, 128), 1) // CAP) == (iota((N_DEV, 128), 0) % GROUP)
    wanted &= iota((N_DEV, 128), 1) < SLOTS
    answers = []
    by_rank = ones_at(
        (iota((8, 128), 1) % CAP == iota((8, 128), 0)) & (iota((8, 128), 1) < SLOTS)
    )
    for s in range(OWN):
        values = jnp.where(wanted, ret_in[:, s, :], 0.0)
        hi, mid, lo = split3(values)
        answers.append(dot_t(by_rank, hi) + dot_t(by_rank, mid) + dot_t(by_rank, lo))
    answers = jnp.concatenate(answers, axis=0)
    hi, mid, lo = split3(answers)
    spread = dot(hi, pick[...]) + dot(mid, pick[...]) + dot(lo, pick[...])
    ids = ids_ref[...]
    row = (ids & 1) * 8 + rank[...].astype(jnp.int32)
    out_ref[...] = jnp.sum(
        jnp.where(iota((16, ROWS), 0) == row, spread, 0.0), axis=0, keepdims=True
    )

    others = pl.ds(0, N_DEV - 1)
    pltpu.make_async_copy(send.at[others], send.at[others], sent_sem).wait()
    pltpu.make_async_copy(ret_in.at[others], ret_in.at[others], back_sent_sem).wait()


def on_device(embeds, cluster):
    nearest = pl.pallas_call(
        kernel,
        out_shape=jax.ShapeDtypeStruct((1, ROWS), jnp.float32),
        in_specs=[
            pl.BlockSpec(memory_space=pltpu.VMEM),
            pl.BlockSpec(memory_space=pl.ANY),
        ],
        out_specs=pl.BlockSpec(memory_space=pltpu.VMEM),
        scratch_shapes=[
            pltpu.VMEM((ROWS, FEAT), jnp.bfloat16),
            pltpu.VMEM((N_DEV, MSG_R, MSG_C), jnp.bfloat16),
            pltpu.VMEM((N_DEV, MSG_R, MSG_C), jnp.bfloat16),
            pltpu.VMEM((OWN, CHUNKS * STRIDE, FEAT), jnp.bfloat16),
            pltpu.VMEM((OWN, CHUNKS * STRIDE, 128), jnp.float32),
            pltpu.VMEM((OWN, 1, CHUNKS * STRIDE), jnp.float32),
            pltpu.VMEM((1, ROWS), jnp.float32),
            pltpu.VMEM((1, ROWS), jnp.int32),
            pltpu.VMEM((N_DEV, ROWS), jnp.bfloat16),
            pltpu.VMEM((4, GROUP * MSG_R, OWN * SLOTS), jnp.bfloat16),
            pltpu.VMEM((4, OWN * STRIDE, GROUP * MSG_R), jnp.bfloat16),
            pltpu.VMEM((CHUNKS, OWN, 128), jnp.float32),
            pltpu.VMEM((N_DEV, OWN, 128), jnp.float32),
            pltpu.SemaphoreType.DMA,
            pltpu.SemaphoreType.DMA,
            pltpu.SemaphoreType.DMA((CHUNKS,)),
            pltpu.SemaphoreType.REGULAR,
            pltpu.SemaphoreType.DMA,
            pltpu.SemaphoreType.DMA,
        ],
        compiler_params=pltpu.CompilerParams(
            collective_id=0, has_side_effects=True, vmem_limit_bytes=48 * 1024 * 1024
        ),
    )(cluster.reshape(1, ROWS), embeds)
    return nearest.reshape(ROWS)


def solution(mesh):
    return jax.shard_map(
        on_device,
        mesh=mesh,
        in_specs=(P(("grp", "dev"), None), P(("grp", "dev"), None)),
        out_specs=P(("grp", "dev")),
        check_vma=False,
    )
```

time: 265 us -> 106 us (0.40)
  waiting for transfers between devices: 119 us -> 0 us
  Pallas kernels: 0 us -> 103 us
  local copies, waits for them, and re-layouts: 53 us -> 2.89 us
  starting transfers between devices: 35.6 us -> 0 us
  other arithmetic: 24.6 us -> 0 us
  matrix products: 24.2 us -> 0 us
  blocking collectives: 6.53 us -> 0 us
    all_to_all x5 -> x0, waiting for transfers between devices: 119 us -> none  [the longest x1 70 us: on_device(): lax.all_to_all(lax.all_to_all(send_rows, 'grp', split_axis=0, concat_axis...]
    pallas_call x0 -> x1, Pallas kernels: none -> 103 us  [on_device(): pl.pallas_call(kernel, out_shape=jax.ShapeDtypeStruct((1, ROWS), jnp.floa...]
    all_to_all x5 -> x0, starting transfers between devices: 35.6 us -> none  [the longest x1 14.4 us: on_device(): lax.all_to_all(lax.all_to_all(send_counts, 'grp', split_axis=0, concat_ax...]
    dot_general x4 -> x0, matrix products: 24.2 us -> none  [tile_max(): lax.dot_general(block_rows, flat_rows, (((1,), (1,)), ((), ())), preferre...]
    gather x1 -> x0, local copies, waits for them, and re-layouts: 20.5 us -> none  [on_device(): return returned.reshape(total_slots)[target]]
    reshape x8 -> x0, local copies, waits for them, and re-layouts: 15.1 us -> none  [the longest x2 8.33 us: on_device(): send_rows = send_rows.reshape(grp_count, dev_count, slot_count, feat_count)]
    scatter x1 -> x0, other arithmetic: 11.8 us -> none  [on_device(): jnp.zeros((device_count * slot_count, feat_count), jnp.bfloat16).at[target]]
    all_to_all x8 -> x0, local copies, waits for them, and re-layouts: 10.2 us -> none  [the longest x1 4.09 us: on_device(): lax.all_to_all(send_rows, 'grp', split_axis=0, concat_axis=0, tiled=True)]
  transfers between devices with their start and end apart: 5 -> 0, of which waited for: 4 -> 0; matrix products, arithmetic and copies ran while one was open for 14% -> 0% of each run, Pallas kernels for 0% -> 0%
where the time goes in v1:
time: 106 us
  Pallas kernels  103 us (97%)
  local copies, waits for them, and re-layouts  2.89 us (3%)
    pallas_call x1, Pallas kernels, on_device(): pl.pallas_call(kernel, out_shape=jax.ShapeDtypeStruct((1, ROWS), jnp.floa...  103 us
    unnamed x5, local copies, waits for them, and re-layouts  2.89 us

profile of v1, /device:TPU:1, one launch (start us, length us, event | category | flops | bytes accessed | tf_op | source)
XLA Modules:
  0.0 106.1 jit_solution(4773594398509853352)
XLA Ops:
  0.0 0.0 copy-start
  0.0 1.6 %copy-done = bf16[2048,512]{1,0:T(8,128)(2,1)S(1)} copy-done((bf16[2048,512]{1,0:T(8,128)(2,1)S(1)}, bf16[2048,512]{1,0:T(8,128)(2,1)}, u32[]{:S(2)}) %copy-start) | copy-done | bytes 2097176
  1.6 0.0 copy-start.1
  1.6 0.7 copy-done.1
  2.3 103.2 %shard_map.28 = f32[1,2048]{1,0:T(1,128)S(1)} custom-call(s32[1,2048]{1,0:T(1,128)S(1)} %bitcast.3, bf16[2048,512]{1,0:T(8,128)(2,1)S(1)} %copy-done), custom_call_target="tpu_custom_call" | custom-call | tf_op jit(solution)/shard_map/pallas_call | solution.py:262
  105.5 0.6 copy.4
Async XLA Ops:
  0.0 1.6 %copy-start = (bf16[2048,512]{1,0:T(8,128)(2,1)S(1)}, bf16[2048,512]{1,0:T(8,128)(2,1)}, u32[]{:S(2)}) copy-start(bf16[2048,512]{1,0:T(8,128)(2,1)} %embeds_hbm.1) | copy-start | bytes 6291460
  1.6 0.7 copy-start.1

commit v2 on v1

--- a/solution.py
+++ b/solution.py
@@ -17,6 +17,7 @@
 CHUNKS = N_DEV // GROUP
 SLOTS = GROUP * CAP
 STRIDE = 128
+HALF = NZ * CAP
 MSG_R, MSG_C = 16, 384
 HEAD = 384
 DEAD = 4.0
@@ -49,8 +50,8 @@
 
 def kernel(
     ids_ref, embeds_hbm, out_ref,
-    embeds, send, recv, unit, bias, best, rank, place, pick,
-    pack, unpack, ret_out, ret_in,
+    embeds, send, recv, unit, bias, best, rank, pick,
+    pack, unpack, tri, wanted, back_out, back_mid, back_half, back_in,
     load_sem, sent_sem, got_sem, in_sem, back_sent_sem, back_got_sem,
 ):
     my_y = lax.axis_index("grp")
@@ -83,23 +84,11 @@
             barrier, inc=1, device_id=column(g, 1) + near[0], device_id_type=LOGICAL
         )
 
-    tri = ones_at(
+    tri[...] = ones_at(
         (iota((128, 256), 0) < iota((128, 256), 1)) | (iota((128, 256), 1) >= 128)
     )
 
-    def rank_block(b, seen):
-        at = pl.ds(pl.multiple_of(b * 128, 128), 128)
-        member = iota((N_CL, 128), 0) == ids_ref[:, at]
-        sums = dot(ones_at(member), tri)
-        rank[:, at] = jnp.sum(
-            jnp.where(member, sums[:, :128] + seen, 0.0), axis=0, keepdims=True
-        )
-        return seen + sums[:, 128:]
-
-    lax.fori_loop(0, ROWS // 128, rank_block, jnp.zeros((N_CL, 128), jnp.float32))
-
     ids = ids_ref[...]
-    ranks = rank[...].astype(jnp.int32)
     owner = ids >> 1
     sub = ids & 1
     dy = ((owner >> 6) - my_y) & (NY - 1)
@@ -108,8 +97,7 @@
     dc = (owner - my_c) & (NC - 1)
     chunk = dy * NX + dx
     member_of = dc * NZ + dz
-    slot = sub * SLOTS + member_of * CAP + ranks
-    place[...] = chunk * (OWN * SLOTS) + slot
+    rank[...] = jnp.zeros((1, ROWS), jnp.int32)
 
     def block_matrix(rows, slots_dim, which):
         block = iota(rows, 1 - slots_dim)
@@ -125,17 +113,28 @@
     for which in range(4):
         peer, q, ok, s = block_matrix((GROUP * MSG_R, OWN * SLOTS), 1, which)
         pack[which] = ones_at(ok & (s == (q // CAP) * SLOTS + peer * CAP + q % CAP))
-        peer, q, ok, s = block_matrix((OWN * STRIDE, GROUP * MSG_R), 0, which)
-        unpack[which] = ones_at(ok & (s == (q // CAP) * STRIDE + peer * CAP + q % CAP))
-
-    pl.semaphore_wait(barrier, GROUP - 1 + CHUNKS - 1)
-    for g in range(1, CHUNKS):
-        pl.semaphore_signal(in_sem, inc=1, device_id=column(g, 1) + near[0], device_id_type=LOGICAL)
-    pl.semaphore_wait(in_sem, CHUNKS - 1)
-    load.wait()
 
     def make_chunk(g):
-        hit = iota((OWN * SLOTS, ROWS), 0) == place[...] - g * (OWN * SLOTS)
+        mine = chunk == g
+        member = iota((OWN * GROUP, ROWS), 0) == jnp.where(mine, sub * GROUP + member_of, -1)
+        blocks = [slice(b * 128, (b + 1) * 128) for b in range(ROWS // 128)]
+        flags = ones_at(member)
+        sums = dot(jnp.concatenate([flags[:, b] for b in blocks], axis=0), tri[...])
+        seen = jnp.zeros((OWN * GROUP, 128), jnp.float32)
+        ranks = []
+        for n, b in enumerate(blocks):
+            part = sums[n * OWN * GROUP : (n + 1) * OWN * GROUP]
+            ranks.append(
+                jnp.sum(
+                    jnp.where(member[:, b], part[:, :128] + seen, 0.0), axis=0, keepdims=True
+                )
+            )
+            seen = seen + part[:, 128:]
+        ranks = jnp.concatenate(ranks, axis=1).astype(jnp.int32)
+        rank[...] += ranks
+        place = jnp.where(mine, sub * SLOTS + member_of * CAP + ranks, -1)
+
+        hit = iota((OWN * SLOTS, ROWS), 0) == place
         chosen = jnp.where(hit, 1.0, 0.0)
         live = jnp.sum(chosen, axis=1, keepdims=True)
         rows = dot(chosen.astype(jnp.bfloat16), embeds[...])
@@ -159,9 +158,15 @@
                 device_id=base + near[j], device_id_type=LOGICAL,
             ).start()
 
+    pl.semaphore_wait(barrier, GROUP - 1 + CHUNKS - 1)
+    for g in range(1, CHUNKS):
+        pl.semaphore_signal(in_sem, inc=1, device_id=column(g, 1) + near[0], device_id_type=LOGICAL)
+    load.wait()
     make_chunk(0)
     send_chunk(0, 1)
     pltpu.make_async_copy(send.at[0], recv.at[0], got_sem.at[0]).start()
+
+    pl.semaphore_wait(in_sem, CHUNKS - 1)
 
     def send_step(g, carry):
         make_chunk(g)
@@ -172,9 +177,18 @@
 
     for s in range(OWN):
         unit[s] = jnp.zeros((CHUNKS * STRIDE, FEAT), jnp.bfloat16)
-        bias[s] = jnp.full((CHUNKS * STRIDE, 128), FAR, jnp.float32)
+        bias[s] = jnp.full((1, CHUNKS * STRIDE), FAR, jnp.float32)
         best[s] = jnp.full((1, CHUNKS * STRIDE), -1.0, jnp.float32)
-    pick[...] = ones_at(iota((N_DEV, ROWS), 0) == chunk * GROUP + member_of)
+    for which in range(4):
+        peer, q, ok, s = block_matrix((OWN * STRIDE, GROUP * MSG_R), 0, which)
+        unpack[which] = ones_at(ok & (s == (q // CAP) * STRIDE + peer * CAP + q % CAP))
+    pick[...] = ones_at(iota((N_DEV, ROWS), 0) == member_of * CHUNKS + chunk)
+    lane = iota((N_DEV, 128), 1)
+    wanted[...] = jnp.where(
+        ((lane % HALF) // CAP == (iota((N_DEV, 128), 0) // CHUNKS) % NZ) & (lane < OWN * HALF),
+        1.0,
+        0.0,
+    )
 
     def got_step(g, carry):
         mine = pl.ds(g * GROUP, GROUP)
@@ -192,20 +206,23 @@
             new = jnp.concatenate([head[part], tail[part]], axis=1).astype(jnp.bfloat16)
             empty = (head[part, :1] > 2.0) | (iota((STRIDE, 1), 0) >= SLOTS)
             new_bias = jnp.where(empty, FAR, 0.0)
-            held = unit[s]
-            by_old = jnp.max(dot_t(held, new) + bias[s], axis=0, keepdims=True)
-            by_new = jnp.max(dot_t(new, held) + new_bias, axis=0, keepdims=True)
-            among = dot_t(new, new) + new_bias
-            among = jnp.where(
-                iota((STRIDE, STRIDE), 0) == iota((STRIDE, STRIDE), 1), -1.0, among
-            )
+            same = iota((STRIDE, STRIDE), 0) == iota((STRIDE, STRIDE), 1)
+            new_row = jnp.sum(jnp.where(same, new_bias, 0.0), axis=0, keepdims=True)
+            sims = dot_t(new, unit[s])
+            by_new = jnp.max(sims + new_bias, axis=0, keepdims=True)
+            by_old = jnp.full((STRIDE, STRIDE), -1.0, jnp.float32)
+            for h in range(CHUNKS):
+                lanes = slice(h * STRIDE, (h + 1) * STRIDE)
+                by_old = jnp.maximum(by_old, sims[:, lanes] + bias[s, :, lanes])
+            by_old = jnp.max(by_old.T, axis=0, keepdims=True)
+            among = jnp.where(same, -1.0, dot_t(new, new) + new_bias)
             arrived = iota((1, CHUNKS * STRIDE), 1) < g * STRIDE
             best[s] = jnp.maximum(best[s], jnp.where(arrived, by_new, -1.0))
             best[s, :, at] = jnp.maximum(
                 jnp.maximum(by_old, jnp.max(among, axis=0, keepdims=True)), -1.0
             )
             unit[s, at] = new
-            bias[s, at] = jnp.broadcast_to(new_bias, (STRIDE, 128))
+            bias[s, :, at] = new_row
         return carry
 
     lax.fori_loop(0, CHUNKS, got_step, 0)
@@ -213,49 +230,48 @@
     far = plane(-1)
     for s in range(OWN):
         for g in range(CHUNKS):
-            ret_out[g, s : s + 1] = best[s, :, g * STRIDE : (g + 1) * STRIDE]
-
-    def return_chunk(g, first):
-        base = column(g, -1)
-        for j in range(first, GROUP):
-            pltpu.make_async_remote_copy(
-                src_ref=ret_out.at[g], dst_ref=ret_in.at[g * GROUP + j],
-                send_sem=back_sent_sem, recv_sem=back_got_sem,
-                device_id=base + far[j], device_id_type=LOGICAL,
-            ).start()
-
-    pltpu.make_async_copy(ret_out.at[0], ret_in.at[0], back_got_sem).start()
-    return_chunk(0, 1)
-
-    def return_step(g, carry):
-        return_chunk(g, 0)
-        return carry
-
-    lax.fori_loop(1, CHUNKS, return_step, 0)
-    pltpu.make_async_copy(ret_in, ret_in, back_got_sem).wait()
-
-    wanted = (iota((N_DEV, 128), 1) // CAP) == (iota((N_DEV, 128), 0) % GROUP)
-    wanted &= iota((N_DEV, 128), 1) < SLOTS
-    answers = []
+            back_out[g, s : s + 1] = best[s, :, g * STRIDE : (g + 1) * STRIDE]
+    for g in range(1, CHUNKS):
+        pltpu.make_async_remote_copy(
+            src_ref=back_out.at[g], dst_ref=back_mid.at[g],
+            send_sem=back_sent_sem.at[0], recv_sem=back_got_sem.at[0],
+            device_id=column(g, -1) + far[0], device_id_type=LOGICAL,
+        ).start()
+    back_mid[0] = back_out[0]
+    rest = pl.ds(1, CHUNKS - 1)
+    pltpu.make_async_copy(back_mid.at[rest], back_mid.at[rest], back_got_sem.at[0]).wait()
+    lane = iota((CHUNKS, 128), 1)
+    first, second = back_mid[:, 0, :], back_mid[:, 1, :]
+    back_half[0] = jnp.where(lane < HALF, first, pltpu.roll(second, HALF, 1))
+    back_half[1] = jnp.where(lane < HALF, pltpu.roll(first, 128 - HALF, 1), second)
+    for j in range(1, GROUP):
+        pltpu.make_async_remote_copy(
+            src_ref=back_half.at[j // NZ], dst_ref=back_in.at[j],
+            send_sem=back_sent_sem.at[1], recv_sem=back_got_sem.at[1],
+            device_id=here + far[j], device_id_type=LOGICAL,
+        ).start()
+    back_in[0] = back_half[0]
+    rest = pl.ds(1, GROUP - 1)
+    pltpu.make_async_copy(back_in.at[rest], back_in.at[rest], back_got_sem.at[1]).wait()
+
+    at_row, at_lane = iota((16, 128), 0), iota((16, 128), 1)
     by_rank = ones_at(
-        (iota((8, 128), 1) % CAP == iota((8, 128), 0)) & (iota((8, 128), 1) < SLOTS)
-    )
-    for s in range(OWN):
-        values = jnp.where(wanted, ret_in[:, s, :], 0.0)
-        hi, mid, lo = split3(values)
-        answers.append(dot_t(by_rank, hi) + dot_t(by_rank, mid) + dot_t(by_rank, lo))
-    answers = jnp.concatenate(answers, axis=0)
+        (at_lane < OWN * HALF) & (at_row == at_lane // HALF * 8 + at_lane % HALF % CAP)
+    )
+    values = jnp.where(wanted[...] > 0.5, back_in[...].reshape(N_DEV, 128), 0.0)
+    hi, mid, lo = split3(values)
+    answers = dot_t(by_rank, hi) + dot_t(by_rank, mid) + dot_t(by_rank, lo)
     hi, mid, lo = split3(answers)
     spread = dot(hi, pick[...]) + dot(mid, pick[...]) + dot(lo, pick[...])
-    ids = ids_ref[...]
-    row = (ids & 1) * 8 + rank[...].astype(jnp.int32)
+    row = (ids_ref[...] & 1) * 8 + rank[...]
     out_ref[...] = jnp.sum(
         jnp.where(iota((16, ROWS), 0) == row, spread, 0.0), axis=0, keepdims=True
     )
 
     others = pl.ds(0, N_DEV - 1)
     pltpu.make_async_copy(send.at[others], send.at[others], sent_sem).wait()
-    pltpu.make_async_copy(ret_in.at[others], ret_in.at[others], back_sent_sem).wait()
+    pltpu.make_async_copy(back_out.at[rest], back_out.at[rest], back_sent_sem.at[0]).wait()
+    pltpu.make_async_copy(back_in.at[rest], back_in.at[rest], back_sent_sem.at[1]).wait()
 
 
 def on_device(embeds, cluster):
@@ -272,21 +288,24 @@
             pltpu.VMEM((N_DEV, MSG_R, MSG_C), jnp.bfloat16),
             pltpu.VMEM((N_DEV, MSG_R, MSG_C), jnp.bfloat16),
             pltpu.VMEM((OWN, CHUNKS * STRIDE, FEAT), jnp.bfloat16),
-            pltpu.VMEM((OWN, CHUNKS * STRIDE, 128), jnp.float32),
             pltpu.VMEM((OWN, 1, CHUNKS * STRIDE), jnp.float32),
-            pltpu.VMEM((1, ROWS), jnp.float32),
+            pltpu.VMEM((OWN, 1, CHUNKS * STRIDE), jnp.float32),
             pltpu.VMEM((1, ROWS), jnp.int32),
             pltpu.VMEM((N_DEV, ROWS), jnp.bfloat16),
             pltpu.VMEM((4, GROUP * MSG_R, OWN * SLOTS), jnp.bfloat16),
             pltpu.VMEM((4, OWN * STRIDE, GROUP * MSG_R), jnp.bfloat16),
+            pltpu.VMEM((128, 256), jnp.bfloat16),
+            pltpu.VMEM((N_DEV, 128), jnp.float32),
             pltpu.VMEM((CHUNKS, OWN, 128), jnp.float32),
-            pltpu.VMEM((N_DEV, OWN, 128), jnp.float32),
+            pltpu.VMEM((CHUNKS, OWN, 128), jnp.float32),
+            pltpu.VMEM((NC, CHUNKS, 128), jnp.float32),
+            pltpu.VMEM((GROUP, CHUNKS, 128), jnp.float32),
             pltpu.SemaphoreType.DMA,
             pltpu.SemaphoreType.DMA,
             pltpu.SemaphoreType.DMA((CHUNKS,)),
             pltpu.SemaphoreType.REGULAR,
-            pltpu.SemaphoreType.DMA,
-            pltpu.SemaphoreType.DMA,
+            pltpu.SemaphoreType.DMA((2,)),
+            pltpu.SemaphoreType.DMA((2,)),
         ],
         compiler_params=pltpu.CompilerParams(
             collective_id=0, has_side_effects=True, vmem_limit_bytes=48 * 1024 * 1024

time: 106 us -> 100 us (0.943)
  Pallas kernels: 103 us -> 97.4 us
    pallas_call x1, Pallas kernels: 103 us -> 97.4 us  [on_device(): pl.pallas_call(kernel, out_shape=jax.ShapeDtypeStruct((1, ROWS), jnp.floa...]
where the time goes in v2:
time: 100 us
  Pallas kernels  97.4 us (97%)
  local copies, waits for them, and re-layouts  2.89 us (3%)
    pallas_call x1, Pallas kernels, on_device(): pl.pallas_call(kernel, out_shape=jax.ShapeDtypeStruct((1, ROWS), jnp.floa...  97.4 us
    unnamed x5, local copies, waits for them, and re-layouts  2.89 us

profile of v2, /device:TPU:1, one launch (start us, length us, event | category | flops | bytes accessed | tf_op | source)
XLA Modules:
  0.0 100.3 jit_solution(5672200633843639610)
XLA Ops:
  0.0 0.0 copy-start
  0.0 1.6 %copy-done = bf16[2048,512]{1,0:T(8,128)(2,1)S(1)} copy-done((bf16[2048,512]{1,0:T(8,128)(2,1)S(1)}, bf16[2048,512]{1,0:T(8,128)(2,1)}, u32[]{:S(2)}) %copy-start) | copy-done | bytes 2097176
  1.6 0.0 copy-start.1
  1.6 0.7 copy-done.1
  2.3 97.4 %shard_map.28 = f32[1,2048]{1,0:T(1,128)S(1)} custom-call(s32[1,2048]{1,0:T(1,128)S(1)} %bitcast.3, bf16[2048,512]{1,0:T(8,128)(2,1)S(1)} %copy-done), custom_call_target="tpu_custom_call" | custom-call | tf_op jit(solution)/shard_map/pallas_call | solution.py:278
  99.7 0.6 copy.4
Async XLA Ops:
  0.0 1.6 %copy-start = (bf16[2048,512]{1,0:T(8,128)(2,1)S(1)}, bf16[2048,512]{1,0:T(8,128)(2,1)}, u32[]{:S(2)}) copy-start(bf16[2048,512]{1,0:T(8,128)(2,1)} %embeds_hbm.1) | copy-start | bytes 6291460
  1.6 0.7 copy-start.1

commit v3 on v2

--- a/solution.py
+++ b/solution.py
@@ -22,6 +22,20 @@
 HEAD = 384
 DEAD = 4.0
 FAR = -1e6
+DIRECT = 4
+EXTRA = CAP - DIRECT
+SPILL = 64
+PAIR = 2 * GROUP
+OWNERS = NY * NX * NC
+D_STEPS = N_DEV // PAIR
+E_STEPS = 4
+EARLY = 1
+Z_ORDER = (1, 7, 2, 6, 3, 5, 4)
+AHEAD = 6
+BEFORE = 5
+E_OWN = OWNERS // E_STEPS
+LANES = 128
+WIDTH = (D_STEPS + E_STEPS) * LANES
 
 
 def iota(shape, dim):
@@ -48,7 +62,7 @@
     return hi, mid, lo
 
 
-def kernel(
+def padded_kernel(
     ids_ref, embeds_hbm, out_ref,
     embeds, send, recv, unit, bias, best, rank, pick,
     pack, unpack, tri, wanted, back_out, back_mid, back_half, back_in,
@@ -274,9 +288,407 @@
     pltpu.make_async_copy(back_in.at[rest], back_in.at[rest], back_sent_sem.at[1]).wait()
 
 
-def on_device(embeds, cluster):
-    nearest = pl.pallas_call(
-        kernel,
+def fast_kernel(
+    ids_ref, embeds_hbm, out_ref, over_ref,
+    embeds, send, recv, spill_out, spill_in, tag_out, tag_in, extra_out, extra_in,
+    unit, bias, best, best_rows, rank, pick, undirect, unextra, tri, wanted,
+    back_out, back_mid, back_half, back_in,
+    load_sem, sent_sem, got_sem, in_sem, spill_sem, tag_sem, extra_sent_sem, extra_sem,
+    back_sent_sem, back_got_sem,
+):
+    my_y = lax.axis_index("grp")
+    my_dev = lax.axis_index("dev")
+    my_x = my_dev // (NZ * NC)
+    my_z = (my_dev // NC) % NZ
+    my_c = my_dev % NC
+
+    load = pltpu.make_async_copy(embeds_hbm, embeds, load_sem)
+    load.start()
+
+    def plane(sign):
+        return [
+            (my_z + sign * (j % NZ) + NZ) % NZ * NC + (my_c + j // NZ) % NC for j in range(GROUP)
+        ]
+
+    def column(g, sign):
+        y = (my_y + sign * (g // NX) + NY) % NY
+        x = (my_x + sign * (g % NX) + NX) % NX
+        return (y * NX + x) * (NZ * NC)
+
+    near = plane(1)
+    here = column(0, 1)
+
+    barrier = pltpu.get_barrier_semaphore()
+    for j in range(1, GROUP):
+        pl.semaphore_signal(barrier, inc=1, device_id=here + near[j], device_id_type=LOGICAL)
+    for g in range(1, CHUNKS):
+        pl.semaphore_signal(
+            barrier, inc=1, device_id=column(g, 1) + near[0], device_id_type=LOGICAL
+        )
+
+    tri[...] = ones_at(
+        (iota((128, 256), 0) < iota((128, 256), 1)) | (iota((128, 256), 1) >= 128)
+    )
+
+    ids = ids_ref[...]
+    owner = ids >> 1
+    sub = ids & 1
+    dy = ((owner >> 6) - my_y) & (NY - 1)
+    dx = ((owner >> 4) - my_x) & (NX - 1)
+    dz = ((owner >> 1) - my_z) & (NZ - 1)
+    dc = (owner - my_c) & (NC - 1)
+    chunk = dy * NX + dx
+    member_of = dc * NZ + dz
+    rank[...] = jnp.zeros((1, ROWS), jnp.int32)
+
+    def count_before(key, kinds):
+        member = iota((kinds, ROWS), 0) == key
+        blocks = [slice(b * 128, (b + 1) * 128) for b in range(ROWS // 128)]
+        flags = ones_at(member)
+        sums = dot(jnp.concatenate([flags[:, b] for b in blocks], axis=0), tri[...])
+        seen = jnp.zeros((kinds, 128), jnp.float32)
+        before = []
+        for n, b in enumerate(blocks):
+            part = sums[n * kinds : (n + 1) * kinds]
+            before.append(
+                jnp.sum(
+                    jnp.where(member[:, b], part[:, :128] + seen, 0.0), axis=0, keepdims=True
+                )
+            )
+            seen = seen + part[:, 128:]
+        return jnp.concatenate(before, axis=1).astype(jnp.int32), seen
+
+    def rank_chunk(g):
+        key = jnp.where(chunk == g, sub * GROUP + member_of, -1)
+        rank[...] += count_before(key, OWN * GROUP)[0]
+
+    def chosen_rows(place, amount):
+        chosen = jnp.where(iota((amount, ROWS), 0) == place, 1.0, 0.0)
+        rows = dot(chosen.astype(jnp.bfloat16), embeds[...])
+        rows = rows * lax.rsqrt(jnp.sum(rows * rows, axis=1, keepdims=True) + 1e-06)
+        return chosen, rows
+
+    def mark_empty(rows, chosen):
+        empty = jnp.sum(chosen, axis=1, keepdims=True) < 0.5
+        return jnp.where((iota(rows.shape, 1) == 0) & empty, DEAD, rows)
+
+    def make_direct(first, chunks):
+        order = chunk - first
+        mine = (order >= 0) & (order < chunks) & (rank[...] < DIRECT)
+        slot = ((order * GROUP + member_of) * OWN + sub) * DIRECT + rank[...]
+        chosen, rows = chosen_rows(jnp.where(mine, slot, -1), chunks * GROUP * OWN * DIRECT)
+        rows = mark_empty(rows, chosen).reshape(chunks * GROUP, OWN * DIRECT, FEAT)
+        block = jnp.concatenate([rows[:, :, : FEAT // 2], rows[:, :, FEAT // 2 :]], axis=1)
+        send[pl.ds(first * GROUP, chunks * GROUP)] = block.astype(jnp.bfloat16)
+
+    def send_chunk(g, first, sem):
+        base = column(g, 1)
+        for j in range(first, GROUP):
+            k = g * GROUP + j
+            pltpu.make_async_remote_copy(
+                src_ref=send.at[k], dst_ref=recv.at[k], send_sem=sent_sem, recv_sem=got_sem.at[sem],
+                device_id=base + near[j], device_id_type=LOGICAL,
+            ).start()
+
+    rank_chunk(0)
+    pl.semaphore_wait(barrier, GROUP - 1 + CHUNKS - 1)
+    for g in range(1, CHUNKS):
+        pl.semaphore_signal(in_sem, inc=1, device_id=column(g, 1) + near[0], device_id_type=LOGICAL)
+    load.wait()
+    make_direct(0, 1)
+    send_chunk(0, 1, 0)
+    pltpu.make_async_copy(send.at[0], recv.at[0], got_sem.at[0]).start()
+
+    def rank_step(g, carry):
+        rank_chunk(g)
+        return carry
+
+    def send_step(q, carry):
+        make_direct(2 * q, 2)
+        send_chunk(2 * q, 0, q)
+        send_chunk(2 * q + 1, 0, q)
+        return carry
+
+    rank_chunk(1)
+    pl.semaphore_wait(in_sem, CHUNKS - 1)
+    make_direct(1, 1)
+    send_chunk(1, 0, 0)
+
+    def early_step(q, carry):
+        rank_chunk(2 * q)
+        rank_chunk(2 * q + 1)
+        return send_step(q, carry)
+
+    lax.fori_loop(1, EARLY, early_step, 0)
+    lax.fori_loop(2 * EARLY, CHUNKS, rank_step, 0)
+
+    beyond = rank[...] >= DIRECT
+    spot, totals = count_before(jnp.where(beyond, dz, -1), 2 * NZ)
+    over = jnp.max(totals, axis=(0, 1), keepdims=True) > SPILL
+    over = jnp.where(over, 1.0, 0.0)
+    place = jnp.where(beyond & (spot < SPILL), dz * SPILL + spot, -1)
+    chosen, rows = chosen_rows(place, NZ * SPILL)
+    spill_out[...] = rows.astype(jnp.bfloat16).reshape(NZ, SPILL, FEAT)
+    spill_in[0] = rows[:SPILL].astype(jnp.bfloat16)
+    label = ((chunk * NC + dc) * OWN + sub) * EXTRA + rank[...] - DIRECT + 1
+    labels = jnp.sum(jnp.where(chosen > 0.5, label.astype(jnp.float32), 0.0), axis=1, keepdims=True)
+    same = iota((LANES, LANES), 0) == iota((LANES, LANES), 1)
+    for b in range(NZ * SPILL // LANES):
+        part = labels[b * LANES : (b + 1) * LANES]
+        line = jnp.sum(jnp.where(same, part, 0.0), axis=0, keepdims=True)
+        tag_out[2 * b] = line.astype(jnp.int32)
+        tag_out[2 * b + 1] = pltpu.roll(line, SPILL, 1).astype(jnp.int32)
+    tag_in[0] = tag_out[0]
+    for piece in range(SPILL // MSG_R):
+        for d in Z_ORDER:
+            rows = pl.ds(piece * MSG_R, MSG_R)
+            pltpu.make_async_remote_copy(
+                src_ref=spill_out.at[d, rows], dst_ref=spill_in.at[d, rows],
+                send_sem=spill_sem.at[0], recv_sem=spill_sem.at[1],
+                device_id=here + near[d], device_id_type=LOGICAL,
+            ).start()
+            if piece == 0:
+                pltpu.make_async_remote_copy(
+                    src_ref=tag_out.at[d], dst_ref=tag_in.at[d],
+                    send_sem=tag_sem.at[0], recv_sem=tag_sem.at[1],
+                    device_id=here + near[d], device_id_type=LOGICAL,
+                ).start()
+
+    lax.fori_loop(EARLY, AHEAD, send_step, 0)
+
+    others = pl.ds(1, NZ - 1)
+    pltpu.make_async_copy(spill_in.at[others], spill_in.at[others], spill_sem.at[1]).wait()
+    pltpu.make_async_copy(tag_in.at[others], tag_in.at[others], tag_sem.at[1]).wait()
+    lane = iota((1, LANES), 1)
+    onward = []
+    for b in range(NZ // 2):
+        line = jnp.where(lane < SPILL, tag_in[2 * b], pltpu.roll(tag_in[2 * b + 1], SPILL, 1))
+        at = line - 1
+        at = (at >> 2) * (NZ * OWN * EXTRA) + (2 * b + (lane >> 6)) * (OWN * EXTRA) + (at & 3)
+        onward.append(jnp.where(line > 0, at, -1))
+    onward = jnp.concatenate(onward, axis=1)
+
+    def onward_step(e, carry):
+        amount = E_OWN * NZ * OWN * EXTRA
+        chosen = jnp.where(iota((amount, NZ * SPILL), 0) + e * amount == onward, 1.0, 0.0)
+        rows = dot(chosen.astype(jnp.bfloat16), spill_in[...].reshape(NZ * SPILL, FEAT))
+        rows = mark_empty(rows, chosen).astype(jnp.bfloat16)
+        extra_out[pl.ds(e * E_OWN, E_OWN)] = rows.reshape(E_OWN, NZ * OWN * EXTRA, FEAT)
+        return carry
+
+    lax.fori_loop(0, E_STEPS, onward_step, 0)
+    pltpu.make_async_copy(extra_out.at[0], extra_in.at[0], extra_sem.at[0]).start()
+    for j in range(E_OWN):
+        for e in (1, 3, 2, 0):
+            k = e * E_OWN + j
+            if k > 0:
+                pltpu.make_async_remote_copy(
+                    src_ref=extra_out.at[k], dst_ref=extra_in.at[k],
+                    send_sem=extra_sent_sem, recv_sem=extra_sem.at[e],
+                    device_id=column(k // NC, 1) + near[j % NC * NZ], device_id_type=LOGICAL,
+                ).start()
+
+    lax.fori_loop(AHEAD, D_STEPS, send_step, 0)
+
+    for s in range(OWN):
+        unit[s] = jnp.zeros((WIDTH, FEAT), jnp.bfloat16)
+        bias[s] = jnp.full((1, WIDTH), FAR, jnp.float32)
+        best[s] = jnp.full((1, WIDTH), -1.0, jnp.float32)
+    to, frm = iota((OWN * LANES, PAIR * MSG_R), 0), iota((OWN * LANES, PAIR * MSG_R), 1)
+    slot = to % LANES
+    at = slot // DIRECT * MSG_R + to // LANES * DIRECT + slot % DIRECT
+    undirect[0] = ones_at(frm == at)
+    undirect[1] = ones_at(frm == at + OWN * DIRECT)
+    to, frm = iota((OWN * LANES, OWN * LANES), 0), iota((OWN * LANES, OWN * LANES), 1)
+    slot = to % LANES
+    unextra[...] = ones_at(
+        frm == slot // EXTRA * (OWN * EXTRA) + to // LANES * EXTRA + slot % EXTRA
+    )
+    pick[...] = ones_at(iota((N_DEV, ROWS), 0) == member_of * CHUNKS + chunk)
+    lane = iota((N_DEV, LANES), 1)
+    lane_dz = jnp.where(lane < 64, lane % 32 // DIRECT, lane % 16 // EXTRA)
+    wanted[...] = jnp.where(
+        (lane_dz == (iota((N_DEV, LANES), 0) // CHUNKS) % NZ) & (lane < 96), 1.0, 0.0
+    )
+
+    def compare(t, both):
+        at = pl.ds(pl.multiple_of(t * LANES, LANES), LANES)
+        for s in range(OWN):
+            part = both[s * LANES : (s + 1) * LANES]
+            new = part.astype(jnp.bfloat16)
+            new_bias = jnp.where(part[:, :1] > 2.0, FAR, 0.0)
+            same = iota((LANES, LANES), 0) == iota((LANES, LANES), 1)
+            new_row = jnp.sum(jnp.where(same, new_bias, 0.0), axis=0, keepdims=True)
+            sims = dot_t(new, unit[s])
+            by_new = jnp.max(sims + new_bias, axis=0, keepdims=True)
+            by_old = jnp.full((LANES, LANES), -1.0, jnp.float32)
+            for h in range(D_STEPS + E_STEPS):
+                lanes = slice(h * LANES, (h + 1) * LANES)
+                by_old = jnp.maximum(by_old, sims[:, lanes] + bias[s, :, lanes])
+            by_old = jnp.max(by_old.T, axis=0, keepdims=True)
+            among = jnp.where(same, -1.0, dot_t(new, new) + new_bias)
+            best[s] = jnp.maximum(best[s], jnp.where(bias[s] > -1.0, by_new, -1.0))
+            best[s, :, at] = jnp.maximum(
+                jnp.maximum(by_old, jnp.max(among, axis=0, keepdims=True)), -1.0
+            )
+            unit[s, at] = new
+            bias[s, :, at] = new_row
+
+    def direct_step(q, carry):
+        mine = pl.ds(q * PAIR, PAIR)
+        pltpu.make_async_copy(recv.at[mine], recv.at[mine], got_sem.at[q]).wait()
+        block = recv[mine].reshape(PAIR * MSG_R, FEAT // 2)
+        compare(q, jnp.concatenate([dot(undirect[0], block), dot(undirect[1], block)], axis=1))
+        return carry
+
+    def extra_step(e, carry):
+        mine = pl.ds(e * E_OWN, E_OWN)
+        pltpu.make_async_copy(extra_in.at[mine], extra_in.at[mine], extra_sem.at[e]).wait()
+        block = extra_in[mine].reshape(OWN * LANES, FEAT)
+        compare(D_STEPS + e, dot(unextra[...], block))
+        return carry
+
+    lax.fori_loop(0, BEFORE, direct_step, 0)
+    lax.fori_loop(0, E_STEPS, extra_step, 0)
+    lax.fori_loop(BEFORE, D_STEPS, direct_step, 0)
+
+    far = plane(-1)
+    for s in range(OWN):
+        for t in range(D_STEPS + E_STEPS):
+            best_rows[s, t : t + 1] = best[s, :, t * LANES : (t + 1) * LANES]
+    lane = iota((D_STEPS, LANES), 1)
+    first, second = best_rows[0, :D_STEPS], best_rows[1, :D_STEPS]
+    even = jnp.where(lane < 64, first, pltpu.roll(second, 64, 1))
+    odd = jnp.where(lane < 64, pltpu.roll(first, 64, 1), second)
+    for q in range(D_STEPS):
+        back_out[2 * q, 0:1] = even[q : q + 1]
+        back_out[2 * q + 1, 0:1] = odd[q : q + 1]
+    first, second = best_rows[0, D_STEPS:], best_rows[1, D_STEPS:]
+    for r in range(4):
+        line = jnp.where(
+            lane < 32,
+            first if r == 0 else pltpu.roll(first, 128 - 32 * r, 1),
+            second if r == 1 else pltpu.roll(second, (160 - 32 * r) % 128, 1),
+        )
+        line = jnp.where(lane < 96, line, over)
+        for e in range(E_STEPS):
+            back_out[4 * e + r, 1:2] = line[e : e + 1]
+    for g in range(1, CHUNKS):
+        pltpu.make_async_remote_copy(
+            src_ref=back_out.at[g], dst_ref=back_mid.at[g],
+            send_sem=back_sent_sem.at[0], recv_sem=back_got_sem.at[0],
+            device_id=column(g, -1) + far[0], device_id_type=LOGICAL,
+        ).start()
+    back_mid[0] = back_out[0]
+    rest = pl.ds(1, CHUNKS - 1)
+    pltpu.make_async_copy(back_mid.at[rest], back_mid.at[rest], back_got_sem.at[0]).wait()
+    lane = iota((CHUNKS, LANES), 1)
+    main, more = back_mid[:, 0, :], back_mid[:, 1, :]
+    over = jnp.max(jnp.where(lane < 96, 0.0, more), axis=(0, 1), keepdims=True)
+    for h in range(NC):
+        line = jnp.where(lane < 96, pltpu.roll(more, 48 - 16 * h, 1), over)
+        line = jnp.where(lane < 80, pltpu.roll(more, 64 - 16 * h, 1), line)
+        line = jnp.where(lane < 64, pltpu.roll(main, 96 - 32 * h, 1), line)
+        back_half[h] = jnp.where(lane < 32, main if h == 0 else pltpu.roll(main, 96, 1), line)
+    for j in range(1, GROUP):
+        pltpu.make_async_remote_copy(
+            src_ref=back_half.at[j // NZ], dst_ref=back_in.at[j],
+            send_sem=back_sent_sem.at[1], recv_sem=back_got_sem.at[1],
+            device_id=here + far[j], device_id_type=LOGICAL,
+        ).start()
+    back_in[0] = back_half[0]
+    rest = pl.ds(1, GROUP - 1)
+    pltpu.make_async_copy(back_in.at[rest], back_in.at[rest], back_got_sem.at[1]).wait()
+
+    at_row, lane = iota((16, LANES), 0), iota((16, LANES), 1)
+    kind = jnp.where(
+        lane < 64, lane // 32 * 8 + lane % DIRECT, (lane - 64) // 16 * 8 + DIRECT + lane % EXTRA
+    )
+    by_rank = ones_at((lane < 96) & (at_row == kind))
+    everything = back_in[...].reshape(N_DEV, LANES)
+    values = jnp.where(wanted[...] > 0.5, everything, 0.0)
+    hi, mid, lo = split3(values)
+    answers = dot_t(by_rank, hi) + dot_t(by_rank, mid) + dot_t(by_rank, lo)
+    hi, mid, lo = split3(answers)
+    spread = dot(hi, pick[...]) + dot(mid, pick[...]) + dot(lo, pick[...])
+    row = (ids_ref[...] & 1) * 8 + rank[...]
+    out_ref[...] = jnp.sum(
+        jnp.where(iota((16, ROWS), 0) == row, spread, 0.0), axis=0, keepdims=True
+    )
+    lane = iota((N_DEV, LANES), 1)
+    over = jnp.max(jnp.where(lane < 96, 0.0, everything), axis=(0, 1), keepdims=True)
+    over_ref[...] = jnp.broadcast_to(over, (1, LANES))
+
+    peers = pl.ds(1, N_DEV - 1)
+    pltpu.make_async_copy(send.at[peers], send.at[peers], sent_sem).wait()
+    pltpu.make_async_copy(spill_out.at[others], spill_out.at[others], spill_sem.at[0]).wait()
+    pltpu.make_async_copy(tag_out.at[others], tag_out.at[others], tag_sem.at[0]).wait()
+    peers = pl.ds(1, OWNERS - 1)
+    pltpu.make_async_copy(extra_out.at[peers], extra_out.at[peers], extra_sent_sem).wait()
+    pltpu.make_async_copy(back_out.at[rest], back_out.at[rest], back_sent_sem.at[0]).wait()
+    pltpu.make_async_copy(back_in.at[rest], back_in.at[rest], back_sent_sem.at[1]).wait()
+
+
+def fast_nearest(ids, embeds):
+    bf16, f32, i32 = jnp.bfloat16, jnp.float32, jnp.int32
+    return pl.pallas_call(
+        fast_kernel,
+        out_shape=(
+            jax.ShapeDtypeStruct((1, ROWS), f32),
+            jax.ShapeDtypeStruct((1, LANES), f32),
+        ),
+        in_specs=[
+            pl.BlockSpec(memory_space=pltpu.VMEM),
+            pl.BlockSpec(memory_space=pl.ANY),
+        ],
+        out_specs=(
+            pl.BlockSpec(memory_space=pltpu.VMEM),
+            pl.BlockSpec(memory_space=pltpu.VMEM),
+        ),
+        scratch_shapes=[
+            pltpu.VMEM((ROWS, FEAT), bf16),
+            pltpu.VMEM((N_DEV, MSG_R, FEAT // 2), bf16),
+            pltpu.VMEM((N_DEV, MSG_R, FEAT // 2), bf16),
+            pltpu.VMEM((NZ, SPILL, FEAT), bf16),
+            pltpu.VMEM((NZ, SPILL, FEAT), bf16),
+            pltpu.VMEM((NZ, 1, LANES), i32),
+            pltpu.VMEM((NZ, 1, LANES), i32),
+            pltpu.VMEM((OWNERS, NZ * OWN * EXTRA, FEAT), bf16),
+            pltpu.VMEM((OWNERS, NZ * OWN * EXTRA, FEAT), bf16),
+            pltpu.VMEM((OWN, WIDTH, FEAT), bf16),
+            pltpu.VMEM((OWN, 1, WIDTH), f32),
+            pltpu.VMEM((OWN, 1, WIDTH), f32),
+            pltpu.VMEM((OWN, 2 * D_STEPS, LANES), f32),
+            pltpu.VMEM((1, ROWS), i32),
+            pltpu.VMEM((N_DEV, ROWS), bf16),
+            pltpu.VMEM((2, OWN * LANES, PAIR * MSG_R), bf16),
+            pltpu.VMEM((OWN * LANES, OWN * LANES), bf16),
+            pltpu.VMEM((128, 256), bf16),
+            pltpu.VMEM((N_DEV, LANES), f32),
+            pltpu.VMEM((CHUNKS, OWN, LANES), f32),
+            pltpu.VMEM((CHUNKS, OWN, LANES), f32),
+            pltpu.VMEM((NC, CHUNKS, LANES), f32),
+            pltpu.VMEM((GROUP, CHUNKS, LANES), f32),
+            pltpu.SemaphoreType.DMA,
+            pltpu.SemaphoreType.DMA,
+            pltpu.SemaphoreType.DMA((D_STEPS,)),
+            pltpu.SemaphoreType.REGULAR,
+            pltpu.SemaphoreType.DMA((2,)),
+            pltpu.SemaphoreType.DMA((2,)),
+            pltpu.SemaphoreType.DMA,
+            pltpu.SemaphoreType.DMA((E_STEPS,)),
+            pltpu.SemaphoreType.DMA((2,)),
+            pltpu.SemaphoreType.DMA((2,)),
+        ],
+        compiler_params=pltpu.CompilerParams(
+            collective_id=1, has_side_effects=True, vmem_limit_bytes=48 * 1024 * 1024
+        ),
+    )(ids, embeds)
+
+
+def padded_nearest(ids, embeds):
+    return pl.pallas_call(
+        padded_kernel,
         out_shape=jax.ShapeDtypeStruct((1, ROWS), jnp.float32),
         in_specs=[
             pl.BlockSpec(memory_space=pltpu.VMEM),
@@ -310,7 +722,15 @@
         compiler_params=pltpu.CompilerParams(
             collective_id=0, has_side_effects=True, vmem_limit_bytes=48 * 1024 * 1024
         ),
-    )(cluster.reshape(1, ROWS), embeds)
+    )(ids, embeds)
+
+
+def on_device(embeds, cluster):
+    ids = cluster.reshape(1, ROWS)
+    nearest, over = fast_nearest(ids, embeds)
+    nearest = lax.cond(
+        over[0, 0] > 0.5, lambda: padded_nearest(ids, embeds), lambda: nearest
+    )
     return nearest.reshape(ROWS)
 
 

time: 100 us -> 92 us (0.920)
  Pallas kernels: 97.4 us -> 91 us
  local copies, waits for them, and re-layouts: 2.89 us -> 0.61 us
    pallas_call x1, Pallas kernels: 97.4 us -> 91 us  [fast_nearest(): pl.pallas_call(fast_kernel, out_shape=(jax.ShapeDtypeStruct((1, ROWS), f3...]
    unnamed x5, local copies, waits for them, and re-layouts: 2.89 us -> 0.61 us
where the time goes in v3:
time: 92 us; the launch traced here: 91.8 us
  Pallas kernels  91 us (99%)
    pallas_call x1, Pallas kernels, fast_nearest(): pl.pallas_call(fast_kernel, out_shape=(jax.ShapeDtypeStruct((1, ROWS), f3...  91 us

profile of v3, /device:TPU:1, one launch (start us, length us, event | category | flops | bytes accessed | tf_op | source)
XLA Modules:
  0.0 91.8 jit_solution(9111537432391438548)
XLA Ops:
  0.0 0.0 copy-start
  0.0 0.0 copy-start.1
  0.0 91.0 %shard_map.30 = (f32[1,2048]{1,0:T(1,128)S(1)}, f32[1,128]{1,0:T(1,128)S(1)}) custom-call(s32[1,2048]{1,0:T(1,128)} %bitcast.6, bf16[2048,512]{1,0:T(8,128)(2,1)} %embeds_hbm.1), custom_call_target="tpu_custom_call" | custom-call | tf_op jit(solution)/shard_map/pallas_call | solution.py:634
  91.0 0.0 copy-done
  91.0 0.0 copy-done.1
  91.0 0.2 conditional.1
  91.2 0.6 copy.9
Async XLA Ops:
  0.0 91.0 %copy-start = (bf16[2048,512]{1,0:T(8,128)(2,1)S(1)}, bf16[2048,512]{1,0:T(8,128)(2,1)}, u32[]{:S(2)}) copy-start(bf16[2048,512]{1,0:T(8,128)(2,1)} %embeds_hbm.1) | copy-start | bytes 6291460
  0.0 91.0 %copy-start.1 = (s32[2048,1]{0,1:T(1,128)S(1)}, s32[2048,1]{0,1:T(1,128)}, u32[]{:S(2)}) copy-start(s32[2048,1]{0,1:T(1,128)} %param.5) | copy-start | bytes 24580

commit v4 on v3

--- a/solution.py
+++ b/solution.py
@@ -30,6 +30,7 @@
 D_STEPS = N_DEV // PAIR
 E_STEPS = 4
 EARLY = 1
+MEANWHILE = 12
 Z_ORDER = (1, 7, 2, 6, 3, 5, 4)
 AHEAD = 6
 BEFORE = 5
@@ -390,15 +391,6 @@
                 device_id=base + near[j], device_id_type=LOGICAL,
             ).start()
 
-    rank_chunk(0)
-    pl.semaphore_wait(barrier, GROUP - 1 + CHUNKS - 1)
-    for g in range(1, CHUNKS):
-        pl.semaphore_signal(in_sem, inc=1, device_id=column(g, 1) + near[0], device_id_type=LOGICAL)
-    load.wait()
-    make_direct(0, 1)
-    send_chunk(0, 1, 0)
-    pltpu.make_async_copy(send.at[0], recv.at[0], got_sem.at[0]).start()
-
     def rank_step(g, carry):
         rank_chunk(g)
         return carry
@@ -409,18 +401,19 @@
         send_chunk(2 * q + 1, 0, q)
         return carry
 
+    rank_chunk(0)
     rank_chunk(1)
+    load.wait()
+    make_direct(0, 2)
+    pl.semaphore_wait(barrier, GROUP - 1 + CHUNKS - 1)
+    for g in range(1, CHUNKS):
+        pl.semaphore_signal(in_sem, inc=1, device_id=column(g, 1) + near[0], device_id_type=LOGICAL)
+    send_chunk(0, 1, 0)
+    pltpu.make_async_copy(send.at[0], recv.at[0], got_sem.at[0]).start()
+    lax.fori_loop(2, MEANWHILE, rank_step, 0)
     pl.semaphore_wait(in_sem, CHUNKS - 1)
-    make_direct(1, 1)
     send_chunk(1, 0, 0)
-
-    def early_step(q, carry):
-        rank_chunk(2 * q)
-        rank_chunk(2 * q + 1)
-        return send_step(q, carry)
-
-    lax.fori_loop(1, EARLY, early_step, 0)
-    lax.fori_loop(2 * EARLY, CHUNKS, rank_step, 0)
+    lax.fori_loop(MEANWHILE, CHUNKS, rank_step, 0)
 
     beyond = rank[...] >= DIRECT
     spot, totals = count_before(jnp.where(beyond, dz, -1), 2 * NZ)

time: 92 us -> 89.9 us (0.977)
  Pallas kernels: 91 us -> 88.9 us
    pallas_call x1, Pallas kernels: 91 us -> 88.9 us  [fast_nearest(): pl.pallas_call(fast_kernel, out_shape=(jax.ShapeDtypeStruct((1, ROWS), f3...]
where the time goes in v4:
time: 89.9 us; the launch traced here: 89.7 us
  Pallas kernels  88.9 us (99%)
    pallas_call x1, Pallas kernels, fast_nearest(): pl.pallas_call(fast_kernel, out_shape=(jax.ShapeDtypeStruct((1, ROWS), f3...  88.9 us

profile of v4, /device:TPU:1, one launch (start us, length us, event | category | flops | bytes accessed | tf_op | source)
XLA Modules:
  0.0 89.7 jit_solution(17219496718088874699)
XLA Ops:
  0.0 0.0 copy-start
  0.0 0.0 copy-start.1
  0.0 88.9 %shard_map.30 = (f32[1,2048]{1,0:T(1,128)S(1)}, f32[1,128]{1,0:T(1,128)S(1)}) custom-call(s32[1,2048]{1,0:T(1,128)} %bitcast.6, bf16[2048,512]{1,0:T(8,128)(2,1)} %embeds_hbm.1), custom_call_target="tpu_custom_call" | custom-call | tf_op jit(solution)/shard_map/pallas_call | solution.py:627
  88.9 0.0 copy-done
  88.9 0.0 copy-done.1
  88.9 0.2 conditional.1
  89.1 0.6 copy.9
Async XLA Ops:
  0.0 88.9 %copy-start = (bf16[2048,512]{1,0:T(8,128)(2,1)S(1)}, bf16[2048,512]{1,0:T(8,128)(2,1)}, u32[]{:S(2)}) copy-start(bf16[2048,512]{1,0:T(8,128)(2,1)} %embeds_hbm.1) | copy-start | bytes 6291460
  0.0 88.9 %copy-start.1 = (s32[2048,1]{0,1:T(1,128)S(1)}, s32[2048,1]{0,1:T(1,128)}, u32[]{:S(2)}) copy-start(s32[2048,1]{0,1:T(1,128)} %param.5) | copy-start | bytes 24580

commit v5 on v4

--- a/solution.py
+++ b/solution.py
@@ -33,7 +33,7 @@
 MEANWHILE = 12
 Z_ORDER = (1, 7, 2, 6, 3, 5, 4)
 AHEAD = 6
-BEFORE = 5
+BEFORE = 6
 E_OWN = OWNERS // E_STEPS
 LANES = 128
 WIDTH = (D_STEPS + E_STEPS) * LANES

time: 89.9 us -> 89.1 us (level)
  no operation moved by 1% of the time
where the time goes in v5:
time: 89.1 us; the launch traced here: 89 us
  Pallas kernels  88.1 us (99%)
    pallas_call x1, Pallas kernels, fast_nearest(): pl.pallas_call(fast_kernel, out_shape=(jax.ShapeDtypeStruct((1, ROWS), f3...  88.1 us

profile of v5, /device:TPU:1, one launch (start us, length us, event | category | flops | bytes accessed | tf_op | source)
XLA Modules:
  0.0 89.0 jit_solution(989987375122225977)
XLA Ops:
  0.0 0.0 copy-start
  0.0 0.0 copy-start.1
  0.0 88.1 %shard_map.30 = (f32[1,2048]{1,0:T(1,128)S(1)}, f32[1,128]{1,0:T(1,128)S(1)}) custom-call(s32[1,2048]{1,0:T(1,128)} %bitcast.6, bf16[2048,512]{1,0:T(8,128)(2,1)} %embeds_hbm.1), custom_call_target="tpu_custom_call" | custom-call | tf_op jit(solution)/shard_map/pallas_call | solution.py:627
  88.1 0.0 copy-done
  88.2 0.0 copy-done.1
  88.2 0.2 conditional.1
  88.4 0.6 copy.9
Async XLA Ops:
  0.0 88.1 %copy-start = (bf16[2048,512]{1,0:T(8,128)(2,1)S(1)}, bf16[2048,512]{1,0:T(8,128)(2,1)}, u32[]{:S(2)}) copy-start(bf16[2048,512]{1,0:T(8,128)(2,1)} %embeds_hbm.1) | copy-start | bytes 6291460
  0.0 88.2 %copy-start.1 = (s32[2048,1]{0,1:T(1,128)S(1)}, s32[2048,1]{0,1:T(1,128)}, u32[]{:S(2)}) copy-start(s32[2048,1]{0,1:T(1,128)} %param.5) | copy-start | bytes 24580
